TPU v7x, 32 devices: a whole 2x2x4 slice. The times are simulated.
32 devices in a mesh: shard: 8 (over z, x), replica: 4 (over y, core).
Axes of the slice: x: 2, y: 2, z: 4, core: 2. Of those that a mesh axis runs over, the one named last changes fastest.
Arguments:
- tokens: bfloat16 [128, 197, 512], P(('shard', 'replica')), may hold values from -6 to 6
- routes: int32 [128, 197, 2], P(('shard', 'replica')), may hold values from 0 to 7, all different within a row; in each aligned block of 788 rows (0 to 787, 788 to 1575, ..., all dimensions but the last counted through in order) at most 376 rows name the same one
- live_images: int32 [32], P(('shard', 'replica')), may hold values from 3 to 4, as said below
- cotangent: bfloat16 [128, 197, 512], P(('shard', 'replica')), may hold values from -6 to 6
- norm_one_gain: bfloat16 [512], P('shard'), may hold values from 0.5 to 1.5
- norm_one_bias: bfloat16 [512], P('shard'), may hold values from -1.75 to 1.75
- qkv_weight: bfloat16 [512, 1536], P('shard'), may hold values from -0.25 to 0.25
- query_value_bias: bfloat16 [2, 512], P(None, 'shard'), may hold values from -1.75 to 1.75
- output_weight: bfloat16 [512, 512], P('shard'), may hold values from -2 to 2
- output_bias: bfloat16 [512], P('shard'), may hold values from -1.75 to 1.75
- norm_two_gain: bfloat16 [512], P('shard'), may hold values from 0.5 to 1.5
- norm_two_bias: bfloat16 [512], P('shard'), may hold values from -1.75 to 1.75
- router_weight: bfloat16 [512, 8], P('shard'), may hold values from -0.1875 to 0.1875
- expert_up: bfloat16 [8, 512, 2048], P(None, None, 'shard'), may hold values from -0.25 to 0.25
- expert_up_bias: bfloat16 [8, 2048], P(None, 'shard'), may hold values from -1.75 to 1.75
- expert_down: bfloat16 [8, 2048, 512], P(None, 'shard'), may hold values from -0.5 to 0.5
- expert_down_bias: bfloat16 [8, 512], P(None, 'shard'), may hold values from -1.75 to 1.75
Outputs:
- mixed: bfloat16 [128, 197, 512], P(('shard', 'replica'))
- grad_tokens: bfloat16 [128, 197, 512], P(('shard', 'replica'))
- grad_norm_one_gain: float32 [512], P('shard')
- grad_norm_one_bias: float32 [512], P('shard')
- grad_qkv_weight: float32 [512, 1536], P('shard')
- grad_query_value_bias: float32 [2, 512], P(None, 'shard')
- grad_output_weight: float32 [512, 512], P('shard')
- grad_output_bias: float32 [512], P('shard')
- grad_norm_two_gain: float32 [512], P('shard')
- grad_norm_two_bias: float32 [512], P('shard')
- grad_router_weight: float32 [512, 8], P('shard')
- grad_expert_up: float32 [8, 512, 2048], P(None, None, 'shard')
- grad_expert_up_bias: float32 [8, 2048], P(None, 'shard')
- grad_expert_down: float32 [8, 2048, 512], P(None, 'shard')
- grad_expert_down_bias: float32 [8, 512], P(None, 'shard')
Inputs may be any that keep to these rules, and one draw needn't show every extreme that they name: `routes`: the two experts of a token differ. Among the 788 tokens of one device no expert is named more than 376 times, a bound that some block reaches. `live_images`: each device has 3 or 4 live images; both values occur in every draw.
All inputs are finite; a program needn't handle non-finite values.
Results may differ from a plain program's by a relative error of at most 0.02.
Values may be sent and summed in bfloat16 or wider, within the bound.
No kernel may reach another device: no remote copies, remote signals or barrier semaphores. Data moves between devices by JAX's collectives and lax.ppermute only.
A program may use at most 320 MiB of HBM per device.

v0:
```python
import jax
import jax.numpy as jnp
from jax import lax
from jax.sharding import PartitionSpec as P

HEADS = 8
EXPERTS = 8
TOP = 2
CAP = 376


NORM_EPS = 1e-06


def layer_norm(values, gain_vec, bias_vec):
    center_mean = jnp.mean(values, -1, keepdims=True)
    centered = values - center_mean
    variance = jnp.mean(centered * centered, -1, keepdims=True)
    return centered * lax.rsqrt(variance + NORM_EPS) * gain_vec + bias_vec


def exact_gelu(values):
    return jax.nn.gelu(values, approximate=False)


def router_softmax(values):
    return jax.nn.softmax(values, axis=-1)


def dispatch_slots(route_flat):
    row_count = route_flat.shape[0] // TOP
    one_hot = (route_flat[:, None] == jnp.arange(EXPERTS, dtype=jnp.int32)[None, :]).astype(
        jnp.int32
    )
    before = jnp.cumsum(one_hot, axis=0) - one_hot
    position = jnp.sum(before * one_hot, axis=1)
    slot_ids = route_flat * CAP + position
    owners = jnp.repeat(jnp.arange(row_count, dtype=jnp.int32), TOP)
    slot_table = jnp.full((EXPERTS * CAP,), row_count, jnp.int32).at[slot_ids].set(owners)
    return (slot_ids, slot_table)


def attention_scores(queries, keys_all, scale_factor):
    return (
        jnp.einsum("ilhd,imhd->ihlm", queries, keys_all, preferred_element_type=jnp.float32)
        * scale_factor
    )


def local(
    tokens,
    routes,
    live_images,
    cotangent,
    norm_one_gain,
    norm_one_bias,
    qkv_weight,
    query_value_bias,
    output_weight,
    output_bias,
    norm_two_gain,
    norm_two_bias,
    router_weight,
    expert_up,
    expert_up_bias,
    expert_down,
    expert_down_bias,
):
    dense_full = (
        lax.all_gather(norm_one_gain, "shard", axis=0, tiled=True),
        lax.all_gather(norm_one_bias, "shard", axis=0, tiled=True),
        lax.all_gather(qkv_weight, "shard", axis=0, tiled=True),
        lax.all_gather(query_value_bias, "shard", axis=1, tiled=True),
        lax.all_gather(output_weight, "shard", axis=0, tiled=True),
        lax.all_gather(output_bias, "shard", axis=0, tiled=True),
        lax.all_gather(norm_two_gain, "shard", axis=0, tiled=True),
        lax.all_gather(norm_two_bias, "shard", axis=0, tiled=True),
        lax.all_gather(router_weight, "shard", axis=0, tiled=True),
        lax.all_gather(expert_down_bias, "shard", axis=1, tiled=True),
    )
    expert_full = (
        lax.all_gather(expert_up, "shard", axis=2, tiled=True),
        lax.all_gather(expert_up_bias, "shard", axis=1, tiled=True),
        lax.all_gather(expert_down, "shard", axis=1, tiled=True),
    )
    (
        gain_one,
        bias_one,
        qkv_full,
        qv_full,
        out_full,
        out_bias_full,
        gain_two,
        bias_two,
        router_full,
        down_bias_full,
    ) = dense_full
    up_full, up_bias_full, down_full = expert_full
    images_here, seq_len, model_width = tokens.shape
    row_count = images_here * seq_len
    head_size = model_width // HEADS
    scale_factor = head_size ** (-0.5)
    float_tokens = tokens.astype(jnp.float32)
    normed_one, norm_one_back = jax.vjp(
        layer_norm, float_tokens, gain_one.astype(jnp.float32), bias_one.astype(jnp.float32)
    )
    first_in = normed_one.astype(jnp.bfloat16).reshape(row_count, model_width)
    projected = jnp.dot(first_in, qkv_full, preferred_element_type=jnp.float32)
    projected = projected.reshape(images_here, seq_len, 3, HEADS, head_size)
    qv_float = qv_full.astype(jnp.float32)
    queries = (projected[:, :, 0] + qv_float[0].reshape(HEADS, head_size)).astype(jnp.bfloat16)
    keys_all = projected[:, :, 1].astype(jnp.bfloat16)
    values_all = (projected[:, :, 2] + qv_float[1].reshape(HEADS, head_size)).astype(jnp.bfloat16)
    scores = attention_scores(queries, keys_all, scale_factor)
    score_top = jnp.max(scores, axis=-1, keepdims=True)
    log_total = score_top + jnp.log(jnp.sum(jnp.exp(scores - score_top), axis=-1, keepdims=True))
    soft_low = jnp.exp(scores - log_total).astype(jnp.bfloat16)
    attended = jnp.einsum(
        "ihlm,imhd->ilhd", soft_low, values_all, preferred_element_type=jnp.float32
    )
    attended = attended.reshape(row_count, model_width).astype(jnp.bfloat16)
    branch = jnp.dot(attended, out_full, preferred_element_type=jnp.float32) + out_bias_full.astype(
        jnp.float32
    )
    middle = float_tokens.reshape(row_count, model_width) + branch
    normed_two, norm_two_back = jax.vjp(
        layer_norm, middle, gain_two.astype(jnp.float32), bias_two.astype(jnp.float32)
    )
    hidden_in = normed_two.astype(jnp.bfloat16)
    hidden_float = hidden_in.astype(jnp.float32)
    logits = jnp.dot(hidden_in, router_full, preferred_element_type=jnp.float32)
    router_probs, softmax_back = jax.vjp(router_softmax, logits)
    route_rows = routes.reshape(row_count, TOP)
    gate_values = jnp.take_along_axis(router_probs, route_rows, axis=1)
    slot_ids, slot_table = dispatch_slots(route_rows.reshape(-1))
    padded = jnp.concatenate([hidden_in, jnp.zeros((1, model_width), jnp.bfloat16)], axis=0)
    expert_rows = padded[slot_table].reshape(EXPERTS, CAP, model_width)
    pre_act = jnp.einsum("ecd,edf->ecf", expert_rows, up_full, preferred_element_type=jnp.float32)
    pre_act = pre_act + up_bias_full.astype(jnp.float32)[:, None, :]
    activated, gelu_back = jax.vjp(exact_gelu, pre_act)
    active_low = activated.astype(jnp.bfloat16)
    expert_result = jnp.einsum(
        "ecf,efd->ecd", active_low, down_full, preferred_element_type=jnp.float32
    )
    expert_result = expert_result + down_bias_full.astype(jnp.float32)[:, None, :]
    picked = expert_result.reshape(EXPERTS * CAP, model_width)[slot_ids].reshape(
        row_count, TOP, model_width
    )
    mixture = jnp.sum(gate_values[:, :, None] * picked, axis=1)
    keep_images = (jnp.arange(images_here, dtype=jnp.int32) < live_images[0]).astype(jnp.float32)
    row_keep = jnp.repeat(keep_images, seq_len)[:, None]
    mixed = (
        ((middle + mixture) * row_keep)
        .astype(jnp.bfloat16)
        .reshape(images_here, seq_len, model_width)
    )
    dense_full = (
        lax.all_gather(norm_one_gain, "shard", axis=0, tiled=True),
        lax.all_gather(norm_one_bias, "shard", axis=0, tiled=True),
        lax.all_gather(qkv_weight, "shard", axis=0, tiled=True),
        lax.all_gather(query_value_bias, "shard", axis=1, tiled=True),
        lax.all_gather(output_weight, "shard", axis=0, tiled=True),
        lax.all_gather(output_bias, "shard", axis=0, tiled=True),
        lax.all_gather(norm_two_gain, "shard", axis=0, tiled=True),
        lax.all_gather(norm_two_bias, "shard", axis=0, tiled=True),
        lax.all_gather(router_weight, "shard", axis=0, tiled=True),
        lax.all_gather(expert_down_bias, "shard", axis=1, tiled=True),
    )
    expert_full = (
        lax.all_gather(expert_up, "shard", axis=2, tiled=True),
        lax.all_gather(expert_up_bias, "shard", axis=1, tiled=True),
        lax.all_gather(expert_down, "shard", axis=1, tiled=True),
    )
    qkv_full = dense_full[2]
    out_full = dense_full[4]
    router_float = dense_full[8].astype(jnp.float32)
    up_full = expert_full[0]
    down_full = expert_full[2]
    dtotal = cotangent.astype(jnp.float32).reshape(row_count, model_width) * row_keep
    grad_gates = jnp.sum(dtotal[:, None, :] * picked, axis=-1)
    dresult_rows = (gate_values[:, :, None] * dtotal[:, None, :]).reshape(
        row_count * TOP, model_width
    )
    dresult = jnp.zeros((EXPERTS * CAP, model_width), jnp.float32).at[slot_ids].set(dresult_rows)
    dresult = dresult.astype(jnp.bfloat16).reshape(EXPERTS, CAP, model_width)
    grad_down_bias = jnp.sum(dresult, axis=1, dtype=jnp.float32)
    grad_down = jnp.einsum("ecf,ecd->efd", active_low, dresult, preferred_element_type=jnp.float32)
    dactive = jnp.einsum("ecd,efd->ecf", dresult, down_full, preferred_element_type=jnp.float32)
    dpre = gelu_back(dactive)[0].astype(jnp.bfloat16)
    grad_up_bias = jnp.sum(dpre, axis=1, dtype=jnp.float32)
    grad_up = jnp.einsum("ecd,ecf->edf", expert_rows, dpre, preferred_element_type=jnp.float32)
    dslots = jnp.einsum("ecf,edf->ecd", dpre, up_full, preferred_element_type=jnp.float32)
    dslots = dslots.reshape(EXPERTS * CAP, model_width)
    dhidden = jnp.sum(dslots[slot_ids].reshape(row_count, TOP, model_width), axis=1)
    route_hot = (
        route_rows[:, :, None] == jnp.arange(EXPERTS, dtype=jnp.int32)[None, None, :]
    ).astype(jnp.float32)
    dprobs = jnp.sum(grad_gates[:, :, None] * route_hot, axis=1)
    dlogits = softmax_back(dprobs)[0]
    grad_router = jnp.dot(hidden_float.T, dlogits, precision=lax.Precision.HIGHEST)
    dhidden = dhidden + jnp.dot(dlogits, router_float.T, precision=lax.Precision.HIGHEST)
    dmiddle_norm, grad_gain_two, grad_bias_two = norm_two_back(dhidden)
    dmiddle = dtotal + dmiddle_norm
    dbranch = dmiddle.astype(jnp.bfloat16)
    grad_out_bias = jnp.sum(dbranch, axis=0, dtype=jnp.float32)
    grad_out = jnp.dot(attended.T, dbranch, preferred_element_type=jnp.float32)
    dattended = jnp.dot(dbranch, out_full.T, preferred_element_type=jnp.float32)
    dattended = dattended.astype(jnp.bfloat16).reshape(images_here, seq_len, HEADS, head_size)
    scores_again = attention_scores(queries, keys_all, scale_factor)
    soft_again = jnp.exp(scores_again - log_total)
    soft_again_low = soft_again.astype(jnp.bfloat16)
    dvalues = jnp.einsum(
        "ihlm,ilhd->imhd", soft_again_low, dattended, preferred_element_type=jnp.float32
    )
    dsoft = jnp.einsum("ilhd,imhd->ihlm", dattended, values_all, preferred_element_type=jnp.float32)
    dscores = soft_again * (dsoft - jnp.sum(dsoft * soft_again, axis=-1, keepdims=True))
    dscores = dscores.astype(jnp.bfloat16)
    dqueries = (
        jnp.einsum("ihlm,imhd->ilhd", dscores, keys_all, preferred_element_type=jnp.float32)
        * scale_factor
    )
    dkeys = (
        jnp.einsum("ihlm,ilhd->imhd", dscores, queries, preferred_element_type=jnp.float32)
        * scale_factor
    )
    dprojected = jnp.stack([dqueries, dkeys, dvalues], axis=2).astype(jnp.bfloat16)
    dprojected = dprojected.reshape(row_count, 3 * model_width)
    grad_qv = jnp.stack(
        [
            jnp.sum(dprojected[:, :model_width], axis=0, dtype=jnp.float32),
            jnp.sum(dprojected[:, 2 * model_width :], axis=0, dtype=jnp.float32),
        ]
    )
    grad_qkv = jnp.dot(first_in.T, dprojected, preferred_element_type=jnp.float32)
    dfirst = jnp.dot(dprojected, qkv_full.T, preferred_element_type=jnp.float32)
    dinput_norm, grad_gain_one, grad_bias_one = norm_one_back(
        dfirst.reshape(images_here, seq_len, model_width)
    )
    grad_tokens = (dmiddle.reshape(images_here, seq_len, model_width) + dinput_norm).astype(
        jnp.bfloat16
    )
    dense_shares = (
        lax.psum_scatter(
            grad_gain_one.astype(jnp.bfloat16), "shard", scatter_dimension=0, tiled=True
        ).astype(jnp.float32),
        lax.psum_scatter(
            grad_bias_one.astype(jnp.bfloat16), "shard", scatter_dimension=0, tiled=True
        ).astype(jnp.float32),
        lax.psum_scatter(
            grad_qkv.astype(jnp.bfloat16), "shard", scatter_dimension=0, tiled=True
        ).astype(jnp.float32),
        lax.psum_scatter(
            grad_qv.astype(jnp.bfloat16), "shard", scatter_dimension=1, tiled=True
        ).astype(jnp.float32),
        lax.psum_scatter(
            grad_out.astype(jnp.bfloat16), "shard", scatter_dimension=0, tiled=True
        ).astype(jnp.float32),
        lax.psum_scatter(
            grad_out_bias.astype(jnp.bfloat16), "shard", scatter_dimension=0, tiled=True
        ).astype(jnp.float32),
        lax.psum_scatter(
            grad_gain_two.astype(jnp.bfloat16), "shard", scatter_dimension=0, tiled=True
        ).astype(jnp.float32),
        lax.psum_scatter(
            grad_bias_two.astype(jnp.bfloat16), "shard", scatter_dimension=0, tiled=True
        ).astype(jnp.float32),
        lax.psum_scatter(
            grad_router.astype(jnp.bfloat16), "shard", scatter_dimension=0, tiled=True
        ).astype(jnp.float32),
        lax.psum_scatter(
            grad_down_bias.astype(jnp.bfloat16), "shard", scatter_dimension=1, tiled=True
        ).astype(jnp.float32),
    )
    dense_totals = lax.psum(
        (
            dense_shares[0],
            dense_shares[1],
            dense_shares[2],
            dense_shares[3],
            dense_shares[4],
            dense_shares[5],
            dense_shares[6],
            dense_shares[7],
            dense_shares[8],
            dense_shares[9],
        ),
        "replica",
    )
    shard_sums = (
        lax.psum_scatter(
            grad_up.astype(jnp.bfloat16), "shard", scatter_dimension=2, tiled=True
        ).astype(jnp.float32),
        lax.psum_scatter(
            grad_up_bias.astype(jnp.bfloat16), "shard", scatter_dimension=1, tiled=True
        ).astype(jnp.float32),
        lax.psum_scatter(
            grad_down.astype(jnp.bfloat16), "shard", scatter_dimension=1, tiled=True
        ).astype(jnp.float32),
    )
    expert_totals = (
        lax.psum(shard_sums[0].astype(jnp.bfloat16), "replica").astype(jnp.float32),
        lax.psum(shard_sums[1].astype(jnp.bfloat16), "replica").astype(jnp.float32),
        lax.psum(shard_sums[2].astype(jnp.bfloat16), "replica").astype(jnp.float32),
    )
    return (
        mixed,
        grad_tokens,
        dense_totals[0],
        dense_totals[1],
        dense_totals[2],
        dense_totals[3],
        dense_totals[4],
        dense_totals[5],
        dense_totals[6],
        dense_totals[7],
        dense_totals[8],
        expert_totals[0],
        expert_totals[1],
        expert_totals[2],
        dense_totals[9],
    )


def solution(mesh):
    return jax.shard_map(
        local,
        mesh=mesh,
        in_specs=(
            P(("shard", "replica"), None, None),
            P(("shard", "replica"), None, None),
            P(("shard", "replica")),
            P(("shard", "replica"), None, None),
            P("shard"),
            P("shard"),
            P("shard", None),
            P(None, "shard"),
            P("shard", None),
            P("shard"),
            P("shard"),
            P("shard"),
            P("shard", None),
            P(None, None, "shard"),
            P(None, "shard"),
            P(None, "shard", None),
            P(None, "shard"),
        ),
        out_specs=(
            P(("shard", "replica"), None, None),
            P(("shard", "replica"), None, None),
            P("shard"),
            P("shard"),
            P("shard", None),
            P(None, "shard"),
            P("shard", None),
            P("shard"),
            P("shard"),
            P("shard"),
            P("shard", None),
            P(None, None, "shard"),
            P(None, "shard"),
            P(None, "shard", None),
            P(None, "shard"),
        ),
        check_vma=False,
    )
```

profile of v0, /device:TPU:0, one launch (start us, length us, event | category | flops | bytes accessed | tf_op | source)
XLA Modules:
  0.0 1662.1 jit_solution(123758443916711570)
XLA Ops:
  16.4 23.3 %all-reduce.14 = (bf16[512]{0:T(512)(128)(2,1)S(1)}, bf16[512]{0:T(512)(128)(2,1)S(1)}, bf16[512]{0:T(512)(128)(2,1)S(1)}, bf16[512]{0:T(512)(128)(2,1)S(1)}, bf16[512]{0:T(512)(128)(2,1)S(1)}) all-reduce(bf16[512]{0:T(512)(128)(2,1)S(1)} %dynamic-update-slice.1, ...), channel_id=1, replica_groups=mesh['shard'=8,'replica'=4] {'shard'}, use_global_device_ids=true, to_apply=%add.3 | all-reduce | flops 2560 | bytes 10240
  39.8 16.3 all-gather
  56.3 30.7 %all_gather.54 = bf16[8,2048]{1,0:T(8,128)(2,1)S(1)} all-gather(bf16[8,256]{1,0:T(8,128)(2,1)S(1)} %copy-done.64), channel_id=1, replica_groups=mesh['shard'=8,'replica'=4] {'shard'}, dimensions={1}, use_global_device_ids=true | all-gather | bytes 36864 | tf_op jit(solution)/shard_map/all_gather | solution.py:83
  103.8 29.3 %all-gather.1 = bf16[8,64,8]{1,2,0:T(8,128)(2,1)S(1)} all-gather(bf16[1,64,8]{1,2,0:T(8,128)(2,1)S(1)} %bitcast.152), channel_id=1, replica_groups=mesh['shard'=8,'replica'=4] {'shard'}, dimensions={0}, use_global_device_ids=true | all-gather | bytes 9216 | tf_op jit(solution)/shard_map/all_gather | solution.py:78
  143.5 57.3 %all_gather.48 = bf16[512,512]{1,0:T(8,128)(2,1)S(1)} all-gather(bf16[64,512]{1,0:T(8,128)(2,1)S(1)} %copy-done.39), channel_id=1, replica_groups=mesh['shard'=8,'replica'=4] {'shard'}, dimensions={0}, use_global_device_ids=true | all-gather | bytes 589824 | tf_op jit(solution)/shard_map/all_gather | solution.py:74
  232.3 18.9 %scatter_custom_fusion.1 = f32[3008,512]{1,0:T(8,128)} fusion(s32[1576]{0:T(1024)S(1)} %fusion.41, f32[1576,512]{1,0:T(8,128)} %mul.293, f32[]{:T(128)} %constant.46.clone.1, f32[1576]{0:T(1024)S(1)} %and_select_fusion.1), kind=kCustom, calls=%fused_computation.39 | custom fusion | flops 806912 | bytes 9396228 | tf_op jit(solution)/shard_map/scatter | solution.py:184
  269.7 23.2 %all-gather.9.cloned.1.call-done = bf16[8,512,2048]{2,1,0:T(8,128)(2,1)} async-done(((bf16[8,512,256]{2,1,0:T(8,128)(2,1)}), bf16[8,512,2048]{2,1,0:T(8,128)(2,1)}) %all-gather.9.cloned.1.call-update) | async-done | bytes 16777232 | tf_op jit(solution)/shard_map/all_gather | solution.py:82
  293.0 29.5 %fusion.7 = (u8[376,2048]{1,0:T(8,128)(4,1)}, u8[376,2048]{1,0:T(8,128)(4,1)}, f32[8,376,2048]{2,1,0:T(8,128)}) fusion(f32[8,2048]{1,0:T(8,128)S(1)} %copy-done.27, bf16[8,376,512]{2,1,0:T(8,128)(2,1)} %bitcast.139, bf16[8,512,2048]{2,1,0:T(8,128)(2,1)} %all-gather.9.cloned.1.call-done), kind=kOutput, calls=%fused_computation.35 | convolution fusion | flops 6392938496 | bytes 46104576 | tf_op jit(solution)/shard_map/ecd,edf->ecf/dot_general | solution.py:138
  322.4 199.6 %all-gather.11.cloned.1.call-done = bf16[8,2048,512]{2,1,0:T(8,128)(2,1)} async-done(((bf16[8,256,512]{2,1,0:T(8,128)(2,1)}), bf16[8,2048,512]{2,1,0:T(8,128)(2,1)}) %all-gather.11.cloned.1.call-update) | async-done | bytes 16777232 | tf_op jit(solution)/shard_map/all_gather | solution.py:84
  522.0 71.4 %fusion.51 = (bf16[8,2048]{1,0:T(8,128)(2,1)}, bf16[8,376,2048]{2,1,0:T(8,128)(2,1)}, f32[8,376,2048]{2,1,0:T(8,128)}) fusion(f32[8,376,2048]{2,1,0:T(8,128)} %get-tuple-element.160, f32[8,2048]{1,0:T(8,128)S(1)} %copy-done.27, u8[376,2048]{1,0:T(8,128)(4,1)} %get-tuple-element.106, u8[376,2048]{1,0:T(8,128)(4,1)} %get-tuple-element.105, ...), kind=kOutput, calls=%fused_computation.149 | convolution fusion | flops 6794887168 | bytes 83099648 | tf_op jit(solution)/shard_map/ecd,efd->ecf/dot_general | solution.py:188
  593.5 17.5 %convolution_convert_fusion.1 = bf16[8,512,2048]{2,1,0:T(8,128)(2,1)} fusion(bf16[8,376,512]{2,1,0:T(8,128)(2,1)} %bitcast.140, bf16[8,376,2048]{2,1,0:T(8,128)(2,1)} %get-tuple-element.143), kind=kOutput, calls=%fused_computation.28 | convolution fusion | flops 6316621824 | bytes 32178176 | tf_op jit(solution)/shard_map/ecd,ecf->edf/dot_general | solution.py:191
  611.0 22.0 %multiply_convert_fusion = bf16[8,376,2048]{2,1,0:T(8,128)(2,1)} fusion(f32[8,376,2048]{2,1,0:T(8,128)} %get-tuple-element.144, f32[8,376,2048]{2,1,0:T(8,128)} %get-tuple-element.160, f32[8,2048]{1,0:T(8,128)S(1)} %copy-done.27), kind=kLoop, calls=%fused_computation.14 | loop fusion | flops 24641536 | bytes 61669376 | tf_op jit(solution)/shard_map/convert_element_type | solution.py:141
  649.0 27.2 %all-gather.2 = bf16[8,64,8]{1,2,0:T(8,128)(2,1)S(1)} all-gather(bf16[1,64,8]{1,2,0:T(8,128)(2,1)S(1)} %bitcast.153), channel_id=1, replica_groups=mesh['shard'=8,'replica'=4] {'shard'}, dimensions={0}, use_global_device_ids=true | all-gather | bytes 9216 | tf_op jit(solution)/shard_map/all_gather | solution.py:79
  830.0 62.2 %reduce-scatter.19.cloned.1.call-done = bf16[8,512,256]{2,1,0:T(8,128)(2,1)} async-done(((bf16[8,512,2048]{2,1,0:T(8,128)(2,1)}), bf16[8,512,256]{2,1,0:T(8,128)(2,1)}) %reduce-scatter.19.cloned.1.call-update) | async-done | bytes 2097168 | tf_op jit(solution)/shard_map/reduce_scatter | solution.py:290
  892.2 285.2 %reduce-scatter.23.cloned.1.call-done = bf16[8,256,512]{2,1,0:T(8,128)(2,1)} async-done(((bf16[8,2048,512]{2,1,0:T(8,128)(2,1)}), bf16[8,256,512]{2,1,0:T(8,128)(2,1)}) %reduce-scatter.23.cloned.1.call-update) | async-done | bytes 2097168 | tf_op jit(solution)/shard_map/reduce_scatter | solution.py:296
  1178.1 62.4 %reduce-scatter.29.cloned.1.call-done = bf16[64,8]{1,0:T(8,128)(2,1)} async-done(((bf16[512,8]{1,0:T(8,128)(2,1)}), bf16[64,8]{1,0:T(8,128)(2,1)}) %reduce-scatter.29.cloned.1.call-update) | async-done | bytes 1040
  1244.1 19.8 %all-reduce.13 = (bf16[512]{0:T(512)(128)(2,1)S(1)}, bf16[512]{0:T(512)(128)(2,1)S(1)}, bf16[512]{0:T(512)(128)(2,1)S(1)}, bf16[512]{0:T(512)(128)(2,1)S(1)}, bf16[512]{0:T(512)(128)(2,1)S(1)}) all-reduce(bf16[512]{0:T(512)(128)(2,1)S(1)} %get-tuple-element.113, ...), channel_id=2, replica_groups=mesh['shard'=8,'replica'=4] {'shard'}, use_global_device_ids=true, to_apply=%region_24.25.clone | all-reduce | flops 2560 | bytes 10240
  1264.1 40.2 %reduce-scatter.25.cloned.1.call-done = bf16[64,2]{1,0:T(8,128)(2,1)} async-done(((bf16[512,2]{1,0:T(8,128)(2,1)}), bf16[64,2]{1,0:T(8,128)(2,1)}) %reduce-scatter.25.cloned.1.call-update) | async-done | bytes 272
  1305.1 63.0 %reduce-scatter.27.cloned.1.call-done = bf16[64,8]{1,0:T(8,128)(2,1)} async-done(((bf16[512,8]{1,0:T(8,128)(2,1)}), bf16[64,8]{1,0:T(8,128)(2,1)}) %reduce-scatter.27.cloned.1.call-update) | async-done | bytes 1040
  1368.9 54.9 %reduce-scatter.21.cloned.1.call-done = bf16[8,256]{1,0:T(8,128)(2,1)} async-done(((bf16[8,2048]{1,0:T(8,128)(2,1)}), bf16[8,256]{1,0:T(8,128)(2,1)}) %reduce-scatter.21.cloned.1.call-update) | async-done | bytes 4112 | tf_op jit(solution)/shard_map/reduce_scatter | solution.py:293
  1430.2 57.9 %reduce-scatter.17.cloned.1.call-done = bf16[64,512]{1,0:T(8,128)(2,1)} async-done(((bf16[512,512]{1,0:T(8,128)(2,1)}), bf16[64,512]{1,0:T(8,128)(2,1)}) %reduce-scatter.17.cloned.1.call-update) | async-done | bytes 65552 | tf_op jit(solution)/shard_map/reduce_scatter | solution.py:255
  1488.0 68.2 %reduce-scatter.15.cloned.1.call-done = bf16[64,1536]{1,0:T(8,128)(2,1)} async-done(((bf16[512,1536]{1,0:T(8,128)(2,1)}), bf16[64,1536]{1,0:T(8,128)(2,1)}) %reduce-scatter.15.cloned.1.call-update) | async-done | bytes 196624 | tf_op jit(solution)/shard_map/reduce_scatter | solution.py:249
  1556.2 24.2 %all-reduce.20 = (f32[64]{0:T(128)}, f32[64]{0:T(128)}, f32[64,1536]{1,0:T(8,128)}, f32[2,64]{1,0:T(2,128)}, f32[64,512]{1,0:T(8,128)}, /*index=5*/f32[64]{0:T(1...) all-reduce(f32[64]{0:T(128)S(1)} %dynamic-slice_convert_fusion.4, ...), channel_id=1, replica_groups=mesh['shard'=8,'replica'=4] {'replica'}, use_global_device_ids=true, to_apply=%region_25.26 | all-reduce | flops 132544 | bytes 795904 | tf_op jit(solution)/shard_map/psum | solution.py:274
  1580.4 67.9 %all-reduce.19.cloned.1.call-done = (bf16[8,512,256]{2,1,0:T(8,128)(2,1)}, bf16[8,256,512]{2,1,0:T(8,128)(2,1)}) async-done(((bf16[8,512,256]{2,1,0:T(8,128)(2,1)}, bf16[8,256,512]{2,1,0:T(8,128)(2,1)}), (bf16[8,512,256]{2,1,0:T(8,128)(2,1)}, bf16[8,256,512]{2,1,0:T(8,128)(2,1)})) %all-reduce.19.cloned.1.call-update) | async-done | bytes 4194320 | tf_op jit(solution)/shard_map/psum | solution.py:301
  (332 shorter events, 272.3 us)
Async XLA Ops:
  7.2 80.5 %copy-start.36 = (s32[4,197,2]{1,2,0:T(2,128)S(1)}, s32[4,197,2]{1,2,0:T(2,128)}, u32[]{:S(2)}) copy-start(s32[4,197,2]{1,2,0:T(2,128)} %param.18) | copy-start | bytes 18916
  7.3 193.6 %all-gather.7.cloned.1.call-start = ((), (), s32[]{:S(2)}) async-start(), calls=%async_computation.8 | async-start | bytes 1769472 | tf_op jit(solution)/shard_map/all_gather | solution.py:72
  8.0 284.9 %all-gather.9.cloned.1.call-start = ((), (), s32[]{:S(2)}) async-start(), calls=%async_computation.9 | async-start | bytes 18874368 | tf_op jit(solution)/shard_map/all_gather | solution.py:82
  8.8 513.3 %all-gather.11.cloned.1.call-start = ((), (), s32[]{:S(2)}) async-start(), calls=%async_computation.10 | async-start | bytes 18874368 | tf_op jit(solution)/shard_map/all_gather | solution.py:84
  9.5 882.7 %reduce-scatter.19.cloned.1.call-start = ((), (), s32[]{:S(2)}) async-start(), calls=%async_computation.13 | async-start | bytes 18874368 | tf_op jit(solution)/shard_map/reduce_scatter | solution.py:290
  11.2 122.1 %copy-start.37 = (s32[4,197,2]{1,0,2:T(4,128)}, s32[4,197,2]{1,0,2:T(4,128)S(1)}, u32[]{:S(2)}) copy-start(s32[4,197,2]{1,0,2:T(4,128)S(1)} %copy.159) | copy-start | bytes 18916
  39.8 163.0 %copy-start.62 = (f32[512]{0:T(512)}, f32[512]{0:T(512)S(1)}, u32[]{:S(2)}) copy-start(f32[512]{0:T(512)S(1)} %convert_element_type.196) | copy-start | bytes 6148
  39.8 163.0 %copy-start.60 = (f32[512]{0:T(512)}, f32[512]{0:T(512)S(1)}, u32[]{:S(2)}) copy-start(f32[512]{0:T(512)S(1)} %convert_element_type.195) | copy-start | bytes 6148
  56.2 148.6 %copy-start.46 = (f32[8,64]{1,0:T(8,128)}, f32[8,64]{1,0:T(8,128)S(1)}, u32[]{:S(2)}) copy-start(f32[8,64]{1,0:T(8,128)S(1)} %add.228) | copy-start | bytes 6148
  56.3 151.1 %copy-start.48 = (f32[8,64]{1,0:T(8,128)}, f32[8,64]{1,0:T(8,128)S(1)}, u32[]{:S(2)}) copy-start(f32[8,64]{1,0:T(8,128)S(1)} %add.225) | copy-start | bytes 6148
  56.3 158.6 %copy-start.56 = (f32[512]{0:T(512)}, f32[512]{0:T(512)S(1)}, u32[]{:S(2)}) copy-start(f32[512]{0:T(512)S(1)} %convert_element_type.207) | copy-start | bytes 6148
  133.2 82.1 %copy-start.34 = (bf16[512,8]{0,1:T(8,128)(2,1)}, bf16[512,8]{0,1:T(8,128)(2,1)S(1)}, u32[]{:S(2)}) copy-start(bf16[512,8]{0,1:T(8,128)(2,1)S(1)} %reshape.405) | copy-start | bytes 24580
  133.8 98.4 %copy-start.58 = (s32[1576]{0:T(1024)}, s32[1576]{0:T(1024)S(1)}, u32[]{:S(2)}) copy-start(s32[1576]{0:T(1024)S(1)} %fusion.41) | copy-start | bytes 18916
  143.0 61.8 %copy-start.40 = (f32[4,197]{1,0:T(4,128)}, f32[4,197]{1,0:T(4,128)S(1)}, u32[]{:S(2)}) copy-start(f32[4,197]{1,0:T(4,128)S(1)} %broadcast_multiply_fusion.3) | copy-start | bytes 9460
  292.9 229.1 %copy-start.3 = (bf16[3008,512]{1,0:T(8,128)(2,1)S(1)}, bf16[3008,512]{1,0:T(8,128)(2,1)}, u32[]{:S(2)}) copy-start(bf16[3008,512]{1,0:T(8,128)(2,1)} %convert_element_type.216) | copy-start | bytes 9240580
  611.0 566.4 %reduce-scatter.23.cloned.1.call-start = ((), (), s32[]{:S(2)}) async-start(), calls=%async_computation.15 | async-start | bytes 18874368 | tf_op jit(solution)/shard_map/reduce_scatter | solution.py:296
  648.3 592.2 %reduce-scatter.29.cloned.1.call-start = ((), (), s32[]{:S(2)}) async-start(), calls=%async_computation.18 | async-start | bytes 147456
  679.1 625.1 %reduce-scatter.25.cloned.1.call-start = ((), (), s32[]{:S(2)}) async-start(), calls=%async_computation.16 | async-start | bytes 147456
  803.6 564.5 %reduce-scatter.27.cloned.1.call-start = ((), (), s32[]{:S(2)}) async-start(), calls=%async_computation.17 | async-start | bytes 147456
  806.1 617.7 %reduce-scatter.21.cloned.1.call-start = ((), (), s32[]{:S(2)}) async-start(), calls=%async_computation.14 | async-start | bytes 36864 | tf_op jit(solution)/shard_map/reduce_scatter | solution.py:293
  811.5 676.6 %reduce-scatter.17.cloned.1.call-start = ((), (), s32[]{:S(2)}) async-start(), calls=%async_computation.12 | async-start | bytes 589824 | tf_op jit(solution)/shard_map/reduce_scatter | solution.py:255
  817.6 738.6 %reduce-scatter.15.cloned.1.call-start = ((), (), s32[]{:S(2)}) async-start(), calls=%async_computation.11 | async-start | bytes 1769472 | tf_op jit(solution)/shard_map/reduce_scatter | solution.py:249
  824.9 416.4 %copy-start.21 = (bf16[788,512]{1,0:T(8,128)(2,1)S(1)}, bf16[788,512]{1,0:T(8,128)(2,1)}, u32[]{:S(2)}) copy-start(bf16[788,512]{1,0:T(8,128)(2,1)} %get-tuple-element.149) | copy-start | bytes 2420740
  830.0 818.3 %all-reduce.19.cloned.1.call-start = ((), (), s32[]{:S(2)}) async-start(), calls=%async_computation.19 | async-start | bytes 8388608 | tf_op jit(solution)/shard_map/psum | solution.py:301
  (64 other events, 874.0 us)
Sparse Core Ops, SparseCore 0:
  10.3 46.7 all-gather.6
  59.1 233.7 all-gather.8
  295.1 226.8 all-gather.10
  611.1 281.0 reduce-scatter.18
  896.3 281.0 reduce-scatter.22
  1180.6 59.8 reduce-scatter.28
  1244.4 59.8 reduce-scatter.24
  1308.2 59.8 reduce-scatter.26
  1371.2 52.5 reduce-scatter.20
  1427.0 61.0 reduce-scatter.16
  1492.4 63.7 reduce-scatter.14
  1558.5 89.6 all-reduce.18
where the time goes:
time: 1670 us; the launch traced here: 1660 us
  waiting for transfers between devices  987 us (59%)
  blocking collectives  234 us (14%)
  matrix products  207 us (12%)
  local copies, waits for them, and re-layouts  124 us (7%)
  other arithmetic  92.1 us (6%)
  between operations  17.6 us (1%)
    reduce_scatter x1, waiting for transfers between devices, local(): lax.psum_scatter(grad_down.astype(jnp.bfloat16), 'shard', scatter_dimensi...  285 us
    all_gather x1, waiting for transfers between devices, local(): lax.all_gather(expert_down, 'shard', axis=1, tiled=True)  200 us
    unnamed x15, waiting for transfers between devices  168 us
    dot_general x1, matrix products, local(): jnp.einsum('ecd,efd->ecf', dresult, down_full, preferred_element_type=jnp...  71.4 us
    reduce_scatter x1, waiting for transfers between devices, local(): lax.psum_scatter(grad_qkv.astype(jnp.bfloat16), 'shard', scatter_dimensio...  68.2 us
    psum x1, waiting for transfers between devices, local(): lax.psum(shard_sums[0].astype(jnp.bfloat16), 'replica').astype(jnp.float32)  67.9 us
    reduce_scatter x1, waiting for transfers between devices, local(): lax.psum_scatter(grad_up.astype(jnp.bfloat16), 'shard', scatter_dimension...  62.2 us
    reduce_scatter x1, waiting for transfers between devices, local(): lax.psum_scatter(grad_out.astype(jnp.bfloat16), 'shard', scatter_dimensio...  57.9 us
  transfers between devices with their start and end apart: 12, of which 11 were waited for; matrix products, arithmetic and copies ran while one was open for 19% of the time, Pallas kernels for 0%

commit v1 on v0

v1 whole, which is shorter than its diff:
```python
import functools
import math

import jax
import jax.numpy as jnp
from jax import lax
from jax.experimental import pallas as pl
from jax.experimental.pallas import tpu as pltpu
from jax.sharding import PartitionSpec as P

HEADS = 8
EXPERTS = 8
TOP = 2
NORM_EPS = 1e-06
TILE = 256
SEG = 16
LANES = 128
BF = jnp.bfloat16
F32 = jnp.float32


def layer_norm(values, gain_vec, bias_vec):
    center_mean = jnp.mean(values, -1, keepdims=True)
    centered = values - center_mean
    variance = jnp.mean(centered * centered, -1, keepdims=True)
    return centered * lax.rsqrt(variance + NORM_EPS) * gain_vec + bias_vec


def cycle_order(count):
    if count % 2 or count < 4:
        return list(range(count))
    return list(range(0, count, 2)) + list(range(count - 1, 0, -2))


class Links:
    def __init__(self, shards, copies):
        self.shards, self.copies = shards, copies
        self.team = min(4, copies)
        self.order = cycle_order(shards)
        self.place = [self.order.index(s) for s in range(shards)]
        ring = self.order + self.order[:1]
        self.ahead = [(ring[i], ring[i + 1]) for i in range(shards)]
        self.back = [(b, a) for a, b in self.ahead]
        self.team_bits = [1 << i for i in range(self.team.bit_length() - 1)]
        self.other_bits = []
        bit = self.team
        while bit < copies:
            self.other_bits.append(bit)
            bit *= 2

    def ring_ahead(self, value):
        return lax.ppermute(value, "shard", self.ahead)

    def ring_back(self, value):
        return lax.ppermute(value, "shard", self.back)

    def swap(self, value, bit):
        return lax.ppermute(value, "replica", [(i, i ^ bit) for i in range(self.copies)])

    def my_place(self):
        return jnp.asarray(self.place, jnp.int32)[lax.axis_index("shard")]

    def my_copy(self):
        return lax.axis_index("replica")


def add_low(first, second):
    return (first.astype(F32) + second.astype(F32)).astype(BF)


def expert_kernel(images, experts, chunks, team, meta, *refs):
    hid, cot, posr, posc = refs[:4]
    ups = refs[4 : 4 + chunks]
    downs = refs[4 + chunks : 4 + 2 * chunks]
    ub, db, router = refs[4 + 2 * chunks : 7 + 2 * chunks]
    mix, dhid, gup, gdn, gub, grt, gdb = refs[7 + 2 * chunks : 14 + 2 * chunks]
    xb, tb, ax, xt, tt, at, wu, wd, gu_acc, gd_acc, gb_acc = refs[14 + 2 * chunks :]
    step = pl.program_id(0)
    slots = xt.shape[0]
    tokens = hid.shape[1]
    width = hid.shape[2]
    table = images * experts

    def dot(a, b):
        return lax.dot_general(a, b, (((1,), (0,)), ((), ())), preferred_element_type=F32)

    def dot_nt(a, b):
        return lax.dot_general(a, b, (((1,), (1,)), ((), ())), preferred_element_type=F32)

    def dot_tn(a, b):
        return lax.dot_general(a, b, (((0,), (0,)), ((), ())), preferred_element_type=F32)

    def probabilities(h):
        logits = dot(h, router[...])
        lane = lax.broadcasted_iota(jnp.int32, logits.shape, 1)
        logits = jnp.where(lane < experts, logits, -1e30)
        top = jnp.max(logits, axis=1, keepdims=True)
        e = jnp.exp(logits - top)
        return e / jnp.sum(e, axis=1, keepdims=True)

    @pl.when(step == 0)
    def _():
        grt[...] = jnp.zeros_like(grt)
        gdb[...] = jnp.zeros_like(gdb)
        xt[...] = jnp.zeros_like(xt)
        tt[...] = jnp.zeros_like(tt)
        at[...] = jnp.zeros_like(at)

    @pl.when(step < images)
    def _():
        h = hid[0]
        c = cot[0]
        row = lax.broadcasted_iota(jnp.int32, (slots, tokens), 0)
        pick = (row == posr[0, 0:1, :]) | (row == posr[0, 1:2, :])
        pick = jnp.where(pick, 1.0, 0.0).astype(BF)
        probs = probabilities(h)
        high = probs.astype(BF)
        low = (probs - high.astype(F32)).astype(BF)
        xt[...] = dot(pick, h).astype(BF)
        tt[...] = dot(pick, c).astype(BF)
        at[...] = dot(pick, high) + dot(pick, low)
        for e in range(experts):
            where = step * experts + e
            src = meta[where]
            dst = meta[table + where]

            def copy(k, carry, src=src, dst=dst):
                s = pl.multiple_of(src + k * SEG, SEG)
                d = pl.multiple_of(dst + k * SEG, SEG)
                xb[pl.ds(d, SEG), :] = xt[pl.ds(s, SEG), :]
                tb[pl.ds(d, SEG), :] = tt[pl.ds(s, SEG), :]
                ax[pl.ds(d, SEG), :] = at[pl.ds(s, SEG), :]
                return carry

            lax.fori_loop(0, meta[2 * table + where], copy, 0)

    @pl.when((step >= images) & (step < images + experts))
    def _():
        e = step - images
        start = meta[3 * table + e]
        tiles = meta[3 * table + experts + e]
        used = meta[3 * table + 2 * experts + e]
        part = ups[0].shape[1]
        for k in range(chunks):
            wu[k * part : (k + 1) * part, :] = ups[k][0]
            wd[k * part : (k + 1) * part, :] = downs[k][0]

        def clear(k, carry):
            d = pl.multiple_of(start + used + k * SEG, SEG)
            xb[pl.ds(d, SEG), :] = jnp.zeros((SEG, width), BF)
            tb[pl.ds(d, SEG), :] = jnp.zeros((SEG, width), BF)
            ax[pl.ds(d, SEG), :] = jnp.zeros((SEG, LANES), F32)
            return carry

        lax.fori_loop(0, (tiles * TILE - used) // SEG, clear, 0)
        gu_acc[...] = jnp.zeros_like(gu_acc)
        gd_acc[...] = jnp.zeros_like(gd_acc)
        gb_acc[...] = jnp.zeros_like(gb_acc)

        def tile(j, carry):
            at_row = pl.multiple_of(start + j * TILE, SEG)
            here = pl.ds(at_row, TILE)
            x = xb[here, :]
            t = tb[here, :]
            extra = ax[here, :]
            lane = lax.broadcasted_iota(jnp.int32, extra.shape, 1)
            gate = jnp.sum(jnp.where(lane == e, extra, 0.0), axis=1, keepdims=True)
            pre = dot_nt(x, wu[...]) + ub[0]
            u = 1.0 / (1.0 + (0.3275911 * math.sqrt(0.5)) * jnp.abs(pre))
            bell = jnp.exp(-0.5 * pre * pre)
            poly = 1.421413741 + u * (-1.453152027 + u * 1.061405429)
            poly = u * (0.254829592 + u * (-0.284496736 + u * poly))
            half = (0.5 * poly) * bell
            phi = jnp.where(pre >= 0, 1.0 - half, half)
            active = (pre * phi).astype(BF)
            active_float = active.astype(F32)
            slope = phi + pre * bell * (1.0 / math.sqrt(2.0 * math.pi))
            raw = dot_nt(t, wd[...])
            score = jnp.sum(active_float * raw, axis=1, keepdims=True)
            gated = (gate * active_float).astype(BF)
            dpre = ((gate * raw) * slope).astype(BF)
            gd_acc[...] += dot_tn(gated, t)
            gu_acc[...] += dot_tn(dpre, x)
            gb_acc[...] += dot(jnp.ones((8, TILE), BF), dpre)
            xb[here, :] = dot(gated, wd[...]).astype(BF)
            tb[here, :] = dot(dpre, wu[...]).astype(BF)
            ax[here, :] = jnp.where(lane == e, score, 0.0)
            return carry

        lax.fori_loop(0, tiles, tile, 0)
        for k in range(chunks):
            gup[k, 0] = gu_acc[k * part : (k + 1) * part, :].astype(BF)
            gdn[k, 0] = gd_acc[k * part : (k + 1) * part, :].astype(BF)
        gub[0] = gb_acc[0:1, :]

    @pl.when(step >= images + experts)
    def _():
        image = step - images - experts
        for e in range(experts):
            where = image * experts + e
            dst = meta[where]
            src = meta[table + where]

            def copy(k, carry, src=src, dst=dst):
                s = pl.multiple_of(src + k * SEG, SEG)
                d = pl.multiple_of(dst + k * SEG, SEG)
                xt[pl.ds(d, SEG), :] = xb[pl.ds(s, SEG), :]
                tt[pl.ds(d, SEG), :] = tb[pl.ds(s, SEG), :]
                at[pl.ds(d, SEG), :] = ax[pl.ds(s, SEG), :]
                return carry

            lax.fori_loop(0, meta[2 * table + where], copy, 0)
        h = hid[0]
        c = cot[0]
        probs = probabilities(h)
        lane = lax.broadcasted_iota(jnp.int32, probs.shape, 1)
        routed = (lane == posc[0, :, 2:3]) | (lane == posc[0, :, 3:4])
        gates = (jnp.where(routed, probs, 0.0) * (1.0 / team)).astype(BF)
        slot = lax.broadcasted_iota(jnp.int32, (tokens, slots), 1)
        back = (slot == posc[0, :, 0:1]) | (slot == posc[0, :, 1:2])
        back = jnp.where(back, 1.0, 0.0).astype(BF)
        high = at[...].astype(BF)
        low = (at[...] - high.astype(F32)).astype(BF)
        mix[0] = (dot(back, xt[...]) + dot(gates, db[...])).astype(BF)
        dprobs = dot(back, high) + dot(back, low)
        dprobs = dprobs + jnp.where(routed, dot_nt(c, db[...]) * (1.0 / team), 0.0)
        dlogits = probs * (dprobs - jnp.sum(dprobs * probs, axis=1, keepdims=True))
        dlogits = dlogits.astype(BF)
        dhid[0] = (dot(back, tt[...]) + dot_nt(dlogits, router[...])).astype(BF)
        grt[...] += dot_tn(dlogits, h)
        gdb[...] += dot_tn(gates, c)


def expert_call(hid, cot, routes, ups, downs, up_bias, down_bias, router, team):
    images, tokens, width = hid.shape
    experts, part, _ = ups[0].shape
    chunks = len(ups)
    hidden = part * chunks
    pairs = TOP * tokens
    slots = (pairs + (SEG - 1) * experts) // SEG * SEG
    rows = images * slots + experts * TILE
    rows = (rows + TILE - 1) // TILE * TILE

    choice = (routes[..., None] == jnp.arange(experts, dtype=jnp.int32)).astype(F32)
    hot = jnp.sum(choice, axis=2)
    before = jnp.tril(jnp.ones((tokens, tokens), BF), -1)
    rank = jnp.einsum("ts,ise->ite", before, hot.astype(BF), preferred_element_type=F32)
    count = jnp.sum(hot, axis=1).astype(jnp.int32)
    groups = (count + SEG - 1) // SEG
    padded = groups * SEG
    local_start = jnp.cumsum(padded, axis=1) - padded
    used = jnp.sum(padded, axis=0)
    tiles = (used + TILE - 1) // TILE
    start = (jnp.cumsum(tiles) - tiles) * TILE
    global_start = start[None, :] + jnp.cumsum(padded, axis=0) - padded
    spot = rank + local_start[:, None, :].astype(F32)
    pos = jnp.sum(choice * spot[:, :, None, :], axis=3).astype(jnp.int32)
    posr = jnp.swapaxes(pos, 1, 2)
    posc = jnp.concatenate([pos, routes], axis=2)
    meta = jnp.concatenate(
        [
            local_start.reshape(-1),
            global_start.reshape(-1),
            groups.reshape(-1),
            start,
            tiles,
            used,
        ]
    ).astype(jnp.int32)

    def first(s, m):
        return jnp.where(s < images, s, jnp.clip(s - images - experts, 0, images - 1))

    def middle(s, m):
        return jnp.clip(s - images, 0, experts - 1)

    def last(s, m):
        return jnp.clip(s - images - experts, 0, images - 1)

    weight = pl.BlockSpec((1, part, width), lambda s, m: (middle(s, m), 0, 0))
    token = pl.BlockSpec((1, tokens, width), lambda s, m: (first(s, m), 0, 0))
    whole = lambda shape: pl.BlockSpec(shape, lambda s, m: (0,) * len(shape))
    grid_spec = pltpu.PrefetchScalarGridSpec(
        num_scalar_prefetch=1,
        grid=(2 * images + experts,),
        in_specs=[
            token,
            token,
            pl.BlockSpec((1, TOP, tokens), lambda s, m: (first(s, m), 0, 0)),
            pl.BlockSpec((1, tokens, 2 * TOP), lambda s, m: (first(s, m), 0, 0)),
            *[weight] * (2 * chunks),
            pl.BlockSpec((1, 1, hidden), lambda s, m: (middle(s, m), 0, 0)),
            whole((LANES, width)),
            whole((width, LANES)),
        ],
        out_specs=[
            pl.BlockSpec((1, tokens, width), lambda s, m: (last(s, m), 0, 0)),
            pl.BlockSpec((1, tokens, width), lambda s, m: (last(s, m), 0, 0)),
            pl.BlockSpec((chunks, 1, part, width), lambda s, m: (0, middle(s, m), 0, 0)),
            pl.BlockSpec((chunks, 1, part, width), lambda s, m: (0, middle(s, m), 0, 0)),
            pl.BlockSpec((1, 1, hidden), lambda s, m: (middle(s, m), 0, 0)),
            whole((LANES, width)),
            whole((LANES, width)),
        ],
        scratch_shapes=[
            pltpu.VMEM((rows, width), BF),
            pltpu.VMEM((rows, width), BF),
            pltpu.VMEM((rows, LANES), F32),
            pltpu.VMEM((slots, width), BF),
            pltpu.VMEM((slots, width), BF),
            pltpu.VMEM((slots, LANES), F32),
            pltpu.VMEM((hidden, width), BF),
            pltpu.VMEM((hidden, width), BF),
            pltpu.VMEM((hidden, width), F32),
            pltpu.VMEM((hidden, width), F32),
            pltpu.VMEM((8, hidden), F32),
        ],
    )
    pairs_all = images * pairs
    return pl.pallas_call(
        functools.partial(expert_kernel, images, experts, chunks, team),
        grid_spec=grid_spec,
        out_shape=[
            jax.ShapeDtypeStruct((images, tokens, width), BF),
            jax.ShapeDtypeStruct((images, tokens, width), BF),
            jax.ShapeDtypeStruct((chunks, experts, part, width), BF),
            jax.ShapeDtypeStruct((chunks, experts, part, width), BF),
            jax.ShapeDtypeStruct((experts, 1, hidden), F32),
            jax.ShapeDtypeStruct((LANES, width), F32),
            jax.ShapeDtypeStruct((LANES, width), F32),
        ],
        compiler_params=pltpu.CompilerParams(
            dimension_semantics=("arbitrary",), vmem_limit_bytes=60 * 1024 * 1024
        ),
        cost_estimate=pl.CostEstimate(
            flops=12 * pairs_all * hidden * width + 16 * images * slots * tokens * width,
            bytes_accessed=8 * images * tokens * width + 8 * experts * hidden * width,
            transcendentals=pairs_all * hidden,
        ),
        name="experts",
    )(meta, hid, cot, posr, posc, *ups, *downs, up_bias, down_bias, router)


def gather_team(links, value):
    for bit in reversed(links.team_bits):
        value = jnp.concatenate([value, links.swap(value, bit)], axis=0)
    return value


def reduce_team(links, value):
    for bit in links.team_bits:
        half = value.shape[0] // 2
        value = add_low(value[:half], links.swap(value[half:], bit))
    return value


def gather_quarters(links, value):
    value = value[None]
    for bit in reversed(links.team_bits):
        other = links.swap(value, bit)
        mine_low = (links.my_copy() & bit) == 0
        first = jnp.where(mine_low, value, other)
        second = jnp.where(mine_low, other, value)
        value = jnp.concatenate([first, second], axis=0)
    count = len(links.team_bits)
    shape = value.shape
    value = value.reshape((2,) * count + shape[1:])
    value = jnp.transpose(value, tuple(reversed(range(count))) + tuple(range(count, value.ndim)))
    return value.reshape(shape)


def ring_gather(links, value):
    blocks = [None] * links.shards
    blocks[0] = value
    forward = backward = value
    for j in range(1, links.shards // 2 + 1):
        forward = links.ring_ahead(forward)
        blocks[j] = forward
        if links.shards - j > j:
            backward = links.ring_back(backward)
            blocks[links.shards - j] = backward
    return blocks


def in_shard_order(links, blocks):
    count = links.shards
    stack = jnp.stack(blocks[::-1])
    start = jnp.mod(-links.my_place() - 1, count)
    ring = lax.dynamic_slice_in_dim(jnp.concatenate([stack, stack]), start, count, axis=0)
    return jnp.stack([ring[links.place[s]] for s in range(count)])


def from_shard_order(links, value):
    count = links.shards
    ring = jnp.stack([value[s] for s in links.order])
    return lax.dynamic_slice_in_dim(jnp.concatenate([ring, ring]), links.my_place(), count, axis=0)


def ring_reduce(links, value):
    count = links.shards
    half = count // 2
    total = value[0].astype(F32)
    part = value[half]
    for m in range(half - 1, -1, -1):
        part = links.ring_ahead(part)
        if m:
            part = add_low(part, value[m])
    total = total + part.astype(F32)
    if count > 2:
        part = value[half + 1]
        for m in range(half + 2, count + 1):
            part = links.ring_back(part)
            if m < count:
                part = add_low(part, value[m])
        total = total + part.astype(F32)
    return total


def reduce_dense(links, value):
    shards, team = links.shards, links.team
    rows = value.shape[0] // shards
    value = value.reshape(shards, rows, value.shape[1])
    for bit in links.team_bits:
        half = value.shape[1] // 2
        upper = (links.my_copy() & bit) != 0
        keep = jnp.where(upper, value[:, half:], value[:, :half])
        give = jnp.where(upper, value[:, :half], value[:, half:])
        value = add_low(keep, links.swap(give, bit))
    total = ring_reduce(links, from_shard_order(links, value))
    for bit in links.other_bits:
        total = total + links.swap(total, bit)
    value = total.astype(BF)
    for bit in reversed(links.team_bits):
        other = links.swap(value, bit)
        upper = (links.my_copy() & bit) != 0
        value = jnp.concatenate(
            [jnp.where(upper, other, value), jnp.where(upper, value, other)], axis=0
        )
    return value.astype(F32)


def local(
    links,
    tokens,
    routes,
    live_images,
    cotangent,
    norm_one_gain,
    norm_one_bias,
    qkv_weight,
    query_value_bias,
    output_weight,
    output_bias,
    norm_two_gain,
    norm_two_bias,
    router_weight,
    expert_up,
    expert_up_bias,
    expert_down,
    expert_down_bias,
):
    shards, team = links.shards, links.team
    images_here, seq_len, width = tokens.shape
    row_count = images_here * seq_len
    head_size = width // HEADS
    scale_factor = head_size ** (-0.5)
    d_rows = qkv_weight.shape[0]
    ff_rows = expert_down.shape[1]
    part = ff_rows // team
    member = links.my_copy() % team
    place = links.my_place()

    bias_columns = EXPERTS * ff_rows // d_rows
    columns = [
        router_weight,
        query_value_bias.T,
        norm_one_gain[:, None],
        norm_one_bias[:, None],
        norm_two_gain[:, None],
        norm_two_bias[:, None],
        output_bias[:, None],
        expert_down_bias.T,
        expert_up_bias.reshape(d_rows, bias_columns),
    ]
    sizes = [c.shape[1] for c in columns]
    pad = -sum(sizes) % LANES
    small = jnp.concatenate(columns + [jnp.zeros((d_rows, pad), BF)], axis=1)
    packed = jnp.concatenate([qkv_weight, output_weight, small], axis=1)
    if team > 1:
        half_rows = d_rows // 2
        core = member % 2
        mine = lax.dynamic_slice_in_dim(packed, core * half_rows, half_rows, axis=0)
        full = jnp.stack(ring_gather(links, mine))
        other = links.swap(full, 1)
        low = jnp.where(core == 0, full, other)
        high = jnp.where(core == 0, other, full)
        blocks = jnp.concatenate([low, high], axis=1)
    else:
        blocks = jnp.stack(ring_gather(links, packed))
    full = in_shard_order(links, [blocks[j] for j in range(shards)])
    full = full.reshape(width, packed.shape[1])
    qkv_full = full[:, : 3 * width]
    out_full = full[:, 3 * width : 4 * width]
    offsets = [4 * width]
    for size in sizes:
        offsets.append(offsets[-1] + size)
    cut = [full[:, offsets[i] : offsets[i + 1]] for i in range(len(sizes))]
    router_full = cut[0]
    qv_float = cut[1].astype(F32).T
    gain_one, bias_one, gain_two, bias_two, out_bias = (
        cut[i][:, 0].astype(F32) for i in range(2, 7)
    )
    down_bias_full = cut[7].T
    up_bias_shards = cut[8].reshape(shards, EXPERTS, ff_rows)

    up_part = lax.dynamic_slice_in_dim(expert_up, member * part, part, axis=2)
    up_part = jnp.swapaxes(up_part, 1, 2)
    down_part = lax.dynamic_slice_in_dim(expert_down, member * part, part, axis=1)
    up_part, down_part, blocks = lax.optimization_barrier((up_part, down_part, blocks))
    ups, downs = [up_part], [down_part]
    for _ in range(shards - 1):
        ups.append(links.ring_ahead(ups[-1]))
        downs.append(links.ring_back(downs[-1]))
    downs = [downs[-j % shards] for j in range(shards)]

    keep_images = (jnp.arange(images_here, dtype=jnp.int32) < live_images[0]).astype(F32)
    row_keep = jnp.repeat(keep_images, seq_len)[:, None]
    kept = cotangent * keep_images[:, None, None].astype(BF)
    cot_team = gather_team(links, kept)
    routes_team = gather_team(links, jnp.swapaxes(routes, 1, 2))
    routes_team = jnp.swapaxes(routes_team, 1, 2)

    float_tokens = tokens.astype(F32)
    normed_one, norm_one_back = jax.vjp(layer_norm, float_tokens, gain_one, bias_one)
    first_in = normed_one.astype(BF).reshape(row_count, width)
    projected = jnp.dot(first_in, qkv_full, preferred_element_type=F32)
    projected = projected.reshape(images_here, seq_len, 3, HEADS, head_size)
    queries = (projected[:, :, 0] + qv_float[0].reshape(HEADS, head_size)).astype(BF)
    keys_all = projected[:, :, 1].astype(BF)
    values_all = (projected[:, :, 2] + qv_float[1].reshape(HEADS, head_size)).astype(BF)

    def attention_scores():
        return (
            jnp.einsum("ilhd,imhd->ihlm", queries, keys_all, preferred_element_type=F32)
            * scale_factor
        )

    scores = attention_scores()
    score_top = jnp.max(scores, axis=-1, keepdims=True)
    log_total = score_top + jnp.log(jnp.sum(jnp.exp(scores - score_top), axis=-1, keepdims=True))
    soft_low = jnp.exp(scores - log_total).astype(BF)
    attended = jnp.einsum("ihlm,imhd->ilhd", soft_low, values_all, preferred_element_type=F32)
    attended = attended.reshape(row_count, width).astype(BF)
    branch = jnp.dot(attended, out_full, preferred_element_type=F32) + out_bias
    middle = float_tokens.reshape(row_count, width) + branch
    normed_two, norm_two_back = jax.vjp(layer_norm, middle, gain_two, bias_two)
    hidden_in = normed_two.astype(BF)

    hid_team = gather_team(links, hidden_in.reshape(images_here, seq_len, width))
    up_bias_mine = lax.dynamic_slice_in_dim(up_bias_shards, member * part, part, axis=2)
    up_bias_ahead = from_shard_order(links, up_bias_mine)
    up_bias_rel = jnp.stack([up_bias_ahead[-j % shards] for j in range(shards)])
    up_bias_rel = jnp.swapaxes(up_bias_rel, 0, 1).reshape(EXPERTS, 1, shards * part).astype(F32)
    down_bias_pad = jnp.pad(down_bias_full, ((0, LANES - EXPERTS), (0, 0)))
    router_pad = jnp.pad(router_full, ((0, 0), (0, LANES - EXPERTS)))
    mix_team, dhid_team, gup, gdn, gub, grt, gdb = expert_call(
        hid_team,
        cot_team,
        routes_team,
        ups,
        downs,
        up_bias_rel,
        down_bias_pad,
        router_pad,
        team,
    )

    part_up = gup[shards - 1]
    part_down = gdn[1 % shards]
    for j in range(shards - 2, -1, -1):
        part_up = add_low(links.ring_back(part_up), gup[j])
        part_down = add_low(links.ring_ahead(part_down), gdn[-j % shards])
    for bit in links.other_bits:
        part_up = add_low(part_up, links.swap(part_up, bit))
        part_down = add_low(part_down, links.swap(part_down, bit))

    dhidden = reduce_team(links, dhid_team).astype(F32).reshape(row_count, width)
    mixture = reduce_team(links, mix_team).astype(F32).reshape(row_count, width)
    mixed = ((middle + mixture) * row_keep).astype(BF).reshape(images_here, seq_len, width)

    dtotal = kept.astype(F32).reshape(row_count, width)
    dmiddle_norm, grad_gain_two, grad_bias_two = norm_two_back(dhidden)
    dmiddle = dtotal + dmiddle_norm
    dbranch = dmiddle.astype(BF)
    grad_out_bias = jnp.sum(dbranch, axis=0, dtype=F32)
    grad_out = jnp.dot(attended.T, dbranch, preferred_element_type=F32)
    dattended = jnp.dot(dbranch, out_full.T, preferred_element_type=F32)
    dattended = dattended.astype(BF).reshape(images_here, seq_len, HEADS, head_size)
    soft_again = jnp.exp(attention_scores() - log_total)
    dvalues = jnp.einsum(
        "ihlm,ilhd->imhd", soft_again.astype(BF), dattended, preferred_element_type=F32
    )
    dsoft = jnp.einsum("ilhd,imhd->ihlm", dattended, values_all, preferred_element_type=F32)
    dscores = soft_again * (dsoft - jnp.sum(dsoft * soft_again, axis=-1, keepdims=True))
    dscores = dscores.astype(BF)
    dqueries = (
        jnp.einsum("ihlm,imhd->ilhd", dscores, keys_all, preferred_element_type=F32) * scale_factor
    )
    dkeys = (
        jnp.einsum("ihlm,ilhd->imhd", dscores, queries, preferred_element_type=F32) * scale_factor
    )
    dprojected = jnp.stack([dqueries, dkeys, dvalues], axis=2).astype(BF)
    dprojected = dprojected.reshape(row_count, 3 * width)
    grad_qv = jnp.stack(
        [
            jnp.sum(dprojected[:, :width], axis=0, dtype=F32),
            jnp.sum(dprojected[:, 2 * width :], axis=0, dtype=F32),
        ]
    )
    grad_qkv = jnp.dot(first_in.T, dprojected, preferred_element_type=F32)
    dfirst = jnp.dot(dprojected, qkv_full.T, preferred_element_type=F32)
    dinput_norm, grad_gain_one, grad_bias_one = norm_one_back(
        dfirst.reshape(images_here, seq_len, width)
    )
    grad_tokens = (dmiddle.reshape(images_here, seq_len, width) + dinput_norm).astype(BF)

    gub_rel = jnp.swapaxes(gub.reshape(EXPERTS, shards, part), 0, 1)
    gub_shards = in_shard_order(links, [gub_rel[j] for j in range(shards)])
    gub_full = lax.dynamic_update_slice_in_dim(
        jnp.zeros((shards, EXPERTS, ff_rows), F32), gub_shards, member * part, axis=2
    )
    vectors = jnp.stack(
        [
            *[grt[e] for e in range(EXPERTS)],
            grad_qv[0],
            grad_qv[1],
            grad_gain_one,
            grad_bias_one,
            grad_gain_two,
            grad_bias_two,
            grad_out_bias,
            *[gdb[e] for e in range(EXPERTS)],
        ]
    )
    grad_small = jnp.concatenate(
        [
            vectors.T,
            gub_full.reshape(width, bias_columns),
            jnp.zeros((width, pad), F32),
        ],
        axis=1,
    )
    grad_packed = jnp.concatenate(
        [grad_qkv.astype(BF), grad_out.astype(BF), grad_small.astype(BF)], axis=1
    )
    total = reduce_dense(links, grad_packed)
    share = [total[:, offsets[i] : offsets[i + 1]] for i in range(len(sizes))]

    up_all = gather_quarters(links, part_up)
    down_all = gather_quarters(links, part_down)
    grad_up = jnp.transpose(up_all, (1, 3, 0, 2)).reshape(EXPERTS, width, ff_rows).astype(F32)
    grad_down = jnp.swapaxes(down_all, 0, 1).reshape(EXPERTS, ff_rows, width).astype(F32)
    return (
        mixed,
        grad_tokens,
        share[2][:, 0],
        share[3][:, 0],
        total[:, : 3 * width],
        share[1].T,
        total[:, 3 * width : 4 * width],
        share[6][:, 0],
        share[4][:, 0],
        share[5][:, 0],
        share[0],
        grad_up,
        share[8].reshape(EXPERTS, ff_rows),
        grad_down,
        share[7].T,
    )


def solution(mesh):
    links = Links(mesh.shape["shard"], mesh.shape["replica"])
    both = ("shard", "replica")
    return jax.shard_map(
        functools.partial(local, links),
        mesh=mesh,
        in_specs=(
            P(both, None, None),
            P(both, None, None),
            P(both),
            P(both, None, None),
            P("shard"),
            P("shard"),
            P("shard", None),
            P(None, "shard"),
            P("shard", None),
            P("shard"),
            P("shard"),
            P("shard"),
            P("shard", None),
            P(None, None, "shard"),
            P(None, "shard"),
            P(None, "shard", None),
            P(None, "shard"),
        ),
        out_specs=(
            P(both, None, None),
            P(both, None, None),
            P("shard"),
            P("shard"),
            P("shard", None),
            P(None, "shard"),
            P("shard", None),
            P("shard"),
            P("shard"),
            P("shard"),
            P("shard", None),
            P(None, None, "shard"),
            P(None, "shard"),
            P(None, "shard", None),
            P(None, "shard"),
        ),
        check_vma=False,
    )
```

time: 1670 us -> 564 us (0.34)
  waiting for transfers between devices: 987 us -> 128 us
  blocking collectives: 234 us -> 0 us
  matrix products: 207 us -> 39.5 us
  Pallas kernels: 0 us -> 107 us
  starting transfers between devices: 0.7 us -> 69 us
    reduce_scatter x5 -> x0, waiting for transfers between devices: 528 us -> none  [the longest x1 285 us: local(): lax.psum_scatter(grad_down.astype(jnp.bfloat16), 'shard', scatter_dimensi...]
    all_gather x3 -> x0, waiting for transfers between devices: 223 us -> none  [the longest x1 200 us: local(): lax.all_gather(expert_down, 'shard', axis=1, tiled=True)]
    dot_general x19 -> x11, matrix products: 199 us -> 25.8 us  [the longest x1 4.64 us: local(): dfirst = jnp.dot(dprojected, qkv_full.T, preferred_element_type=F32)]
    unnamed x15 -> x0, waiting for transfers between devices: 168 us -> none
    all_gather x5 -> x0, blocking collectives: 161 us -> none  [the longest x1 57.3 us: local(): lax.all_gather(output_weight, 'shard', axis=0, tiled=True)]
    ppermute x0 -> x61, waiting for transfers between devices: none -> 128 us  [the longest x22 66.4 us: ring_ahead(): return lax.ppermute(value, 'shard', self.ahead)]
    pallas_call x0 -> x1, Pallas kernels: none -> 107 us  [expert_call(): pl.pallas_call(functools.partial(expert_kernel, images, experts, chunks,...]
    ppermute x0 -> x61, starting transfers between devices: none -> 69 us  [the longest x22 37.3 us: ring_ahead(): return lax.ppermute(value, 'shard', self.ahead)]
  transfers between devices with their start and end apart: 12 -> 61, of which waited for: 11 -> 22; matrix products, arithmetic and copies ran while one was open for 19% -> 40% of each run, Pallas kernels for 0% -> 0%
where the time goes in v1:
time: 564 us; the launch traced here: 559 us
  waiting for transfers between devices  128 us (23%)
  local copies, waits for them, and re-layouts  127 us (23%)
  Pallas kernels  107 us (19%)
  other arithmetic  82.9 us (15%)
  starting transfers between devices  69 us (12%)
  matrix products  39.5 us (7%)
    pallas_call x1, Pallas kernels, expert_call(): pl.pallas_call(functools.partial(expert_kernel, images, experts, chunks,...  107 us
    ppermute x22, waiting for transfers between devices, ring_ahead(): return lax.ppermute(value, 'shard', self.ahead)  66.4 us
    ppermute x19, waiting for transfers between devices, swap(): lax.ppermute(value, 'replica', [(i, i ^ bit) for i in range(self.copies)])  49 us
    ppermute x22, starting transfers between devices, ring_ahead(): return lax.ppermute(value, 'shard', self.ahead)  37.3 us
    convert_element_type x20, other arithmetic, add_low(): return (first.astype(F32) + second.astype(F32)).astype(BF)  27.5 us
    unnamed x149, local copies, waits for them, and re-layouts  25.6 us
    ppermute x20, starting transfers between devices, ring_back(): return lax.ppermute(value, 'shard', self.back)  18.3 us
    ppermute x19, starting transfers between devices, swap(): lax.ppermute(value, 'replica', [(i, i ^ bit) for i in range(self.copies)])  13.5 us
  transfers between devices with their start and end apart: 61, of which 22 were waited for; matrix products, arithmetic and copies ran while one was open for 40% of the time, Pallas kernels for 0%

profile of v1, /device:TPU:0, one launch (start us, length us, event | category | flops | bytes accessed | tf_op | source)
XLA Modules:
  0.0 558.7 jit_solution(12787389451184312842)
XLA Ops:
  68.3 6.5 %collective-permute-done.15.refs_6_ = bf16[8,64,512]{2,1,0:T(8,128)(2,1)S(1)} collective-permute-done((bf16[8,64,512]{2,1,0:T(8,128)(2,1)}, bf16[8,64,512]{2,1,0:T(8,128)(2,1)S(1)}, u32[]{:S(2)}, u32[]{:S(2)}) %collective-permute-start.15) | collective-permute-done | bytes 524320 | tf_op jit(solution)/shard_map/ppermute | solution.py:52
  77.5 3.7 pad_add_fusion.refs_3_
  105.9 4.9 fusion.8
  124.2 15.7 %collective-permute-done.10 = bf16[4,197,512]{2,0,1:T(4,128)(2,1)S(1)} collective-permute-done((bf16[4,197,512]{2,0,1:T(4,128)(2,1)S(1)}, bf16[4,197,512]{2,0,1:T(4,128)(2,1)S(1)}, u32[]{:S(2)}, u32[]{:S(2)}) %collective-permute-start.10) | collective-permute-done | bytes 806944 | tf_op jit(solution)/shard_map/ppermute | solution.py:58
  144.1 12.5 %collective-permute-done.18.refs_9_ = bf16[8,64,512]{2,1,0:T(8,128)(2,1)S(1)} collective-permute-done((bf16[8,64,512]{2,1,0:T(8,128)(2,1)}, bf16[8,64,512]{2,1,0:T(8,128)(2,1)S(1)}, u32[]{:S(2)}, u32[]{:S(2)}) %collective-permute-start.18) | collective-permute-done | bytes 524320 | tf_op jit(solution)/shard_map/ppermute | solution.py:52
  159.7 10.5 %collective-permute-done.19.refs_10_ = bf16[8,64,512]{2,1,0:T(8,128)(2,1)} collective-permute-done((bf16[8,64,512]{2,1,0:T(8,128)(2,1)S(1)}, bf16[8,64,512]{2,1,0:T(8,128)(2,1)}, u32[]{:S(2)}, u32[]{:S(2)}) %collective-permute-start.19) | collective-permute-done | bytes 524320 | tf_op jit(solution)/shard_map/ppermute | solution.py:52
  171.9 10.6 %collective-permute-start.27 = (bf16[8,64,512]{2,1,0:T(8,128)(2,1)}, bf16[8,64,512]{2,1,0:T(8,128)(2,1)}, u32[]{:S(2)}, u32[]{:S(2)}) collective-permute-start(bf16[8,64,512]{2,1,0:T(8,128)(2,1)} %collective-permute-done.26.refs_14_), channel_id=1, source_target_pairs={{8,0},{16,8},{24,16},{28,24},{20,28},{12,20},{4,12},{0,4},{9,1},{1... | collective-permute-start | bytes 1572872 | tf_op jit(solution)/shard_map/ppermute | solution.py:55
  194.8 106.9 %experts.1 = (bf16[16,197,512]{2,1,0:T(8,128)(2,1)}, bf16[16,197,512]{2,1,0:T(8,128)(2,1)}, bf16[8,8,64,512]{3,2,1,0:T(8,128)(2,1)}, bf16[8,8,64,512]{3,2,1,0:T(...) custom-call(s32[408]{0:T(512)} %concatenate.80.meta, ...), custom_call_target="tpu_custom_call" | custom-call | flops 33051115520 | bytes 29687808 | tf_op jit(solution)/shard_map/experts/pallas_call | solution.py:320
  318.6 9.2 %collective-permute-done.43 = bf16[8,64,512]{2,1,0:T(8,128)(2,1)} collective-permute-done((bf16[8,64,512]{2,1,0:T(8,128)(2,1)}, bf16[8,64,512]{2,1,0:T(8,128)(2,1)}, u32[]{:S(2)}, u32[]{:S(2)}) %collective-permute-start.43) | collective-permute-done | bytes 524320 | tf_op jit(solution)/shard_map/ppermute | solution.py:55
  344.7 9.2 %collective-permute-done.29 = bf16[4,197,512]{2,0,1:T(4,128)(2,1)S(1)} collective-permute-done((bf16[4,197,512]{2,0,1:T(4,128)(2,1)S(1)}, bf16[4,197,512]{2,0,1:T(4,128)(2,1)S(1)}, u32[]{:S(2)}, u32[]{:S(2)}) %collective-permute-start.29) | collective-permute-done | bytes 806944 | tf_op jit(solution)/shard_map/ppermute | solution.py:58
  358.3 10.9 %collective-permute-done.31 = bf16[4,197,512]{2,0,1:T(4,128)(2,1)} collective-permute-done((bf16[4,197,512]{2,0,1:T(4,128)(2,1)}, bf16[4,197,512]{2,0,1:T(4,128)(2,1)}, u32[]{:S(2)}, u32[]{:S(2)}) %collective-permute-start.31) | collective-permute-done | bytes 806944 | tf_op jit(solution)/shard_map/ppermute | solution.py:58
  381.8 3.6 reshape.499
  388.3 8.7 %multiply_reduce_fusion = (f32[4,8,197]{2,1,0:T(8,128)S(1)}, f32[4,8,197,197]{2,3,1,0:T(8,128)}) fusion(f32[4,8,197,197]{2,3,1,0:T(8,128)} %copy-done.2, f32[4,8,197]{2,1,0:T(8,128)S(1)} %log_add_fusion, bf16[4,197,8,64]{1,3,2,0:T(8,128)(2,1)} %copy.315, f32[4,197,3,8,64]{1,4,3,2,0:T(8,128)} %copy-done.3, f32[8,64]{1,0:T(8,128)S(1)} %add.323), kind=kOutput, calls=%fused_computation.1 | convolution fusion | flops 164729824 | bytes 14719360 | tf_op jit(solution)/shard_map/ilhd,imhd->ihlm/dot_general | solution.py:603
  397.0 6.4 %multiply_convert_fusion = bf16[4,8,197,197]{2,3,1,0:T(8,128)(2,1)S(1)} fusion(f32[4,8,197,197]{2,3,1,0:T(8,128)} %get-tuple-element.194, f32[4,8,197,197]{2,3,1,0:T(8,128)} %copy-done.2, f32[4,8,197]{2,1,0:T(8,128)S(1)} %get-tuple-element.193, f32[4,8,197]{2,1,0:T(8,128)S(1)} %log_add_fusion), kind=kLoop, calls=%fused_computation | loop fusion | flops 6209440 | bytes 12469312 | tf_op jit(solution)/shard_map/convert_element_type | solution.py:605
  410.7 4.5 copy.322
  420.9 6.9 %convert_element_type.576 = bf16[788,1536]{0,1:T(8,128)(2,1)} reshape(bf16[4,197,3,8,64]{1,0,4,3,2:T(4,128)(2,1)} %copy.322) | data formatting | bytes 4841472 | tf_op jit(solution)/shard_map/convert_element_type | solution.py:612
  429.6 4.6 fusion.82
  441.8 3.9 convolution_convert_fusion
  456.2 10.2 %collective-permute-done.55 = bf16[8,64,512]{2,1,0:T(8,128)(2,1)} collective-permute-done((bf16[8,64,512]{2,1,0:T(8,128)(2,1)S(1)}, bf16[8,64,512]{2,1,0:T(8,128)(2,1)}, u32[]{:S(2)}, u32[]{:S(2)}) %collective-permute-start.55) | collective-permute-done | bytes 524320 | tf_op jit(solution)/shard_map/ppermute | solution.py:52
  492.0 5.3 collective-permute-done.57
  503.8 7.9 %collective-permute-done.35 = bf16[16,2176]{1,0:T(8,128)(2,1)S(1)} collective-permute-done((bf16[16,2176]{1,0:T(8,128)(2,1)S(1)}, bf16[16,2176]{1,0:T(8,128)(2,1)S(1)}, u32[]{:S(2)}, u32[]{:S(2)}) %collective-permute-start.35) | collective-permute-done | bytes 69664 | tf_op jit(solution)/shard_map/ppermute | solution.py:52
  521.8 8.0 %collective-permute-done.59 = bf16[1,8,64,512]{3,2,1,0:T(8,128)(2,1)S(1)} collective-permute-done((bf16[1,8,64,512]{3,2,1,0:T(8,128)(2,1)S(1)}, bf16[1,8,64,512]{3,2,1,0:T(8,128)(2,1)S(1)}, u32[]{:S(2)}, u32[]{:S(2)}) %collective-permute-start.59) | collective-permute-done | bytes 524320 | tf_op jit(solution)/shard_map/ppermute | solution.py:58
  532.6 4.1 collective-permute-done.41
  553.0 5.5 copy.334
  (474 shorter events, 273.0 us)
Async XLA Ops:
  9.6 27.0 %collective-permute-start = (bf16[32,2176]{1,0:T(8,128)(2,1)}, bf16[32,2176]{1,0:T(8,128)(2,1)}, u32[]{:S(2)}, u32[]{:S(2)}) collective-permute-start(bf16[32,2176]{1,0:T(8,128)(2,1)} %get-tuple-element.156), channel_id=1, source_target_pairs={{0,8},{8,16},{16,24},{24,28},{28,20},{20,12},{12,4},{4,0},{1,9},{9... | collective-permute-start | bytes 417800 | tf_op jit(solution)/shard_map/ppermute | solution.py:52
  12.6 27.6 %collective-permute-start.4 = (bf16[32,2176]{1,0:T(8,128)(2,1)}, bf16[32,2176]{1,0:T(8,128)(2,1)}, u32[]{:S(2)}, u32[]{:S(2)}) collective-permute-start(bf16[32,2176]{1,0:T(8,128)(2,1)} %get-tuple-element.156), channel_id=1, source_target_pairs={{8,0},{16,8},{24,16},{28,24},{20,28},{12,20},{4,12},{0,4},{9,1},{1... | collective-permute-start | bytes 417800 | tf_op jit(solution)/shard_map/ppermute | solution.py:55
  17.6 42.6 %collective-permute-start.14 = (bf16[8,64,512]{2,1,0:T(8,128)(2,1)S(1)}, bf16[8,64,512]{2,1,0:T(8,128)(2,1)}, u32[]{:S(2)}, u32[]{:S(2)}) collective-permute-start(bf16[8,64,512]{2,1,0:T(8,128)(2,1)S(1)} %bitcast.261), channel_id=1, source_target_pairs={{0,8},{8,16},{16,24},{24,28},{28,20},{20,12},{12,4},{4,0},{1,9},{9... | collective-permute-start | bytes 1572872 | tf_op jit(solution)/shard_map/ppermute | solution.py:52
  19.7 42.3 %collective-permute-start.21 = (bf16[8,64,512]{2,1,0:T(8,128)(2,1)}, bf16[8,64,512]{2,1,0:T(8,128)(2,1)}, u32[]{:S(2)}, u32[]{:S(2)}) collective-permute-start(bf16[8,64,512]{2,1,0:T(8,128)(2,1)} %constant_dynamic-slice_fusion.22.refs_12_), channel_id=1, source_target_pairs={{8,0},{16,8},{24,16},{28,24},{20,28},{12,20},{4,12},{0,4},{9,1},{1... | collective-permute-start | bytes 1572872 | tf_op jit(solution)/shard_map/ppermute | solution.py:55
  35.5 45.7 %collective-permute-start.12 = (bf16[4,197,512]{2,0,1:T(4,128)(2,1)S(1)}, bf16[4,197,512]{2,0,1:T(4,128)(2,1)}, u32[]{:S(2)}, u32[]{:S(2)}) collective-permute-start(bf16[4,197,512]{2,0,1:T(4,128)(2,1)S(1)} %copy.296), channel_id=1, source_target_pairs={{0,2},{1,3},{2,0},{3,1},{4,6},{5,7},{6,4},{7,5},{8,10},{9,11},{10,... | collective-permute-start | bytes 2420744 | tf_op jit(solution)/shard_map/ppermute | solution.py:58
  56.4 34.2 %collective-permute-start.7 = (bf16[8,32,2176]{2,1,0:T(8,128)(2,1)}, bf16[8,32,2176]{2,1,0:T(8,128)(2,1)}, u32[]{:S(2)}, u32[]{:S(2)}) collective-permute-start(bf16[8,32,2176]{2,1,0:T(8,128)(2,1)} %constant_dynamic-update-slice_fusion), channel_id=1, source_target_pairs={{0,1},{1,0},{2,3},{3,2},{4,5},{5,4},{6,7},{7,6},{8,9},{9,8},{10,11... | collective-permute-start | bytes 3342344 | tf_op jit(solution)/shard_map/ppermute | solution.py:58
  85.1 99.6 %collective-permute-start.13 = (bf16[8,197,512]{2,0,1:T(8,128)(2,1)}, bf16[8,197,512]{2,0,1:T(8,128)(2,1)}, u32[]{:S(2)}, u32[]{:S(2)}) collective-permute-start(bf16[8,197,512]{2,0,1:T(8,128)(2,1)} %copy.298), channel_id=1, source_target_pairs={{0,1},{1,0},{2,3},{3,2},{4,5},{5,4},{6,7},{7,6},{8,9},{9,8},{10,11... | collective-permute-start | bytes 4841480 | tf_op jit(solution)/shard_map/ppermute | solution.py:58
  88.6 53.4 %collective-permute-start.17 = (bf16[8,64,512]{2,1,0:T(8,128)(2,1)}, bf16[8,64,512]{2,1,0:T(8,128)(2,1)}, u32[]{:S(2)}, u32[]{:S(2)}) collective-permute-start(bf16[8,64,512]{2,1,0:T(8,128)(2,1)} %collective-permute-done.16.refs_7_), channel_id=1, source_target_pairs={{0,8},{8,16},{16,24},{24,28},{28,20},{20,12},{12,4},{4,0},{1,9},{9... | collective-permute-start | bytes 1572872 | tf_op jit(solution)/shard_map/ppermute | solution.py:52
  90.3 53.4 %collective-permute-start.24 = (bf16[8,64,512]{2,1,0:T(8,128)(2,1)}, bf16[8,64,512]{2,1,0:T(8,128)(2,1)}, u32[]{:S(2)}, u32[]{:S(2)}) collective-permute-start(bf16[8,64,512]{2,1,0:T(8,128)(2,1)} %collective-permute-done.23.refs_17_), channel_id=1, source_target_pairs={{8,0},{16,8},{24,16},{28,24},{20,28},{12,20},{4,12},{0,4},{9,1},{1... | collective-permute-start | bytes 1572872 | tf_op jit(solution)/shard_map/ppermute | solution.py:55
  121.5 18.4 %collective-permute-start.10 = (bf16[4,197,512]{2,0,1:T(4,128)(2,1)S(1)}, bf16[4,197,512]{2,0,1:T(4,128)(2,1)S(1)}, u32[]{:S(2)}, u32[]{:S(2)}) collective-permute-start(bf16[4,197,512]{2,0,1:T(4,128)(2,1)S(1)} %copy.290), channel_id=1, source_target_pairs={{0,2},{1,3},{2,0},{3,1},{4,6},{5,7},{6,4},{7,5},{8,10},{9,11},{10,... | collective-permute-start | bytes 2420744 | tf_op jit(solution)/shard_map/ppermute | solution.py:58
  141.9 46.8 %collective-permute-start.11 = (bf16[8,197,512]{2,0,1:T(8,128)(2,1)}, bf16[8,197,512]{2,0,1:T(8,128)(2,1)}, u32[]{:S(2)}, u32[]{:S(2)}) collective-permute-start(bf16[8,197,512]{2,0,1:T(8,128)(2,1)} %copy.292), channel_id=1, source_target_pairs={{0,1},{1,0},{2,3},{3,2},{4,5},{5,4},{6,7},{7,6},{8,9},{9,8},{10,11... | collective-permute-start | bytes 4841480 | tf_op jit(solution)/shard_map/ppermute | solution.py:58
  170.2 22.5 %collective-permute-start.20 = (bf16[8,64,512]{2,1,0:T(8,128)(2,1)}, bf16[8,64,512]{2,1,0:T(8,128)(2,1)S(1)}, u32[]{:S(2)}, u32[]{:S(2)}) collective-permute-start(bf16[8,64,512]{2,1,0:T(8,128)(2,1)} %collective-permute-done.19.refs_10_), channel_id=1, source_target_pairs={{0,8},{8,16},{16,24},{24,28},{28,20},{20,12},{12,4},{4,0},{1,9},{9... | collective-permute-start | bytes 1572872 | tf_op jit(solution)/shard_map/ppermute | solution.py:52
  171.9 22.9 %collective-permute-start.27 = (bf16[8,64,512]{2,1,0:T(8,128)(2,1)}, bf16[8,64,512]{2,1,0:T(8,128)(2,1)}, u32[]{:S(2)}, u32[]{:S(2)}) collective-permute-start(bf16[8,64,512]{2,1,0:T(8,128)(2,1)} %collective-permute-done.26.refs_14_), channel_id=1, source_target_pairs={{8,0},{16,8},{24,16},{28,24},{20,28},{12,20},{4,12},{0,4},{9,1},{1... | collective-permute-start | bytes 1572872 | tf_op jit(solution)/shard_map/ppermute | solution.py:55
  308.0 26.6 %collective-permute-start.30 = (bf16[8,197,512]{2,0,1:T(8,128)(2,1)}, bf16[8,197,512]{2,0,1:T(8,128)(2,1)}, u32[]{:S(2)}, u32[]{:S(2)}) collective-permute-start(bf16[8,197,512]{2,0,1:T(8,128)(2,1)} %copy.310), channel_id=1, source_target_pairs={{0,1},{1,0},{2,3},{3,2},{4,5},{5,4},{6,7},{7,6},{8,9},{9,8},{10,11... | collective-permute-start | bytes 4841480 | tf_op jit(solution)/shard_map/ppermute | solution.py:58
  309.8 19.9 %collective-permute-start.28 = (bf16[8,197,512]{2,0,1:T(8,128)(2,1)}, bf16[8,197,512]{2,0,1:T(8,128)(2,1)}, u32[]{:S(2)}, u32[]{:S(2)}) collective-permute-start(bf16[8,197,512]{2,0,1:T(8,128)(2,1)} %copy.306), channel_id=1, source_target_pairs={{0,1},{1,0},{2,3},{3,2},{4,5},{5,4},{6,7},{7,6},{8,9},{9,8},{10,11... | collective-permute-start | bytes 4841480 | tf_op jit(solution)/shard_map/ppermute | solution.py:58
  312.2 15.6 %collective-permute-start.43 = (bf16[8,64,512]{2,1,0:T(8,128)(2,1)}, bf16[8,64,512]{2,1,0:T(8,128)(2,1)}, u32[]{:S(2)}, u32[]{:S(2)}) collective-permute-start(bf16[8,64,512]{2,1,0:T(8,128)(2,1)} %slice_bitcast_fusion.4), channel_id=1, source_target_pairs={{8,0},{16,8},{24,16},{28,24},{20,28},{12,20},{4,12},{0,4},{9,1},{1... | collective-permute-start | bytes 1572872 | tf_op jit(solution)/shard_map/ppermute | solution.py:55
  317.4 21.3 %collective-permute-start.53 = (bf16[8,64,512]{2,1,0:T(8,128)(2,1)S(1)}, bf16[8,64,512]{2,1,0:T(8,128)(2,1)S(1)}, u32[]{:S(2)}, u32[]{:S(2)}) collective-permute-start(bf16[8,64,512]{2,1,0:T(8,128)(2,1)S(1)} %fusion.17), channel_id=1, source_target_pairs={{0,8},{8,16},{16,24},{24,28},{28,20},{20,12},{12,4},{4,0},{1,9},{9... | collective-permute-start | bytes 1572872 | tf_op jit(solution)/shard_map/ppermute | solution.py:52
  333.0 21.0 %collective-permute-start.29 = (bf16[4,197,512]{2,0,1:T(4,128)(2,1)S(1)}, bf16[4,197,512]{2,0,1:T(4,128)(2,1)S(1)}, u32[]{:S(2)}, u32[]{:S(2)}) collective-permute-start(bf16[4,197,512]{2,0,1:T(4,128)(2,1)S(1)} %copy.308), channel_id=1, source_target_pairs={{0,2},{1,3},{2,0},{3,1},{4,6},{5,7},{6,4},{7,5},{8,10},{9,11},{10,... | collective-permute-start | bytes 2420744 | tf_op jit(solution)/shard_map/ppermute | solution.py:58
  338.1 31.1 %collective-permute-start.31 = (bf16[4,197,512]{2,0,1:T(4,128)(2,1)}, bf16[4,197,512]{2,0,1:T(4,128)(2,1)}, u32[]{:S(2)}, u32[]{:S(2)}) collective-permute-start(bf16[4,197,512]{2,0,1:T(4,128)(2,1)} %copy.312), channel_id=1, source_target_pairs={{0,2},{1,3},{2,0},{3,1},{4,6},{5,7},{6,4},{7,5},{8,10},{9,11},{10,... | collective-permute-start | bytes 2420744 | tf_op jit(solution)/shard_map/ppermute | solution.py:58
  340.6 109.9 %collective-permute-start.54 = (bf16[8,64,512]{2,1,0:T(8,128)(2,1)}, bf16[8,64,512]{2,1,0:T(8,128)(2,1)}, u32[]{:S(2)}, u32[]{:S(2)}) collective-permute-start(bf16[8,64,512]{2,1,0:T(8,128)(2,1)} %fusion.16), channel_id=1, source_target_pairs={{0,8},{8,16},{16,24},{24,28},{28,20},{20,12},{12,4},{4,0},{1,9},{9... | collective-permute-start | bytes 1572872 | tf_op jit(solution)/shard_map/ppermute | solution.py:52
  344.5 109.3 %collective-permute-start.45 = (bf16[8,64,512]{2,1,0:T(8,128)(2,1)}, bf16[8,64,512]{2,1,0:T(8,128)(2,1)}, u32[]{:S(2)}, u32[]{:S(2)}) collective-permute-start(bf16[8,64,512]{2,1,0:T(8,128)(2,1)} %fusion.23), channel_id=1, source_target_pairs={{8,0},{16,8},{24,16},{28,24},{20,28},{12,20},{4,12},{0,4},{9,1},{1... | collective-permute-start | bytes 1572872 | tf_op jit(solution)/shard_map/ppermute | solution.py:55
  450.5 22.2 %collective-permute-start.32 = (bf16[8,32,2176]{2,1,0:T(8,128)(2,1)S(1)}, bf16[8,32,2176]{2,1,0:T(8,128)(2,1)S(1)}, u32[]{:S(2)}, u32[]{:S(2)}) collective-permute-start(bf16[8,32,2176]{2,1,0:T(8,128)(2,1)S(1)} %broadcast_select_fusion), channel_id=1, source_target_pairs={{0,1},{1,0},{2,3},{3,2},{4,5},{5,4},{6,7},{7,6},{8,9},{9,8},{10,11... | collective-permute-start | bytes 3342344 | tf_op jit(solution)/shard_map/ppermute | solution.py:58
  498.4 15.3 %collective-permute-start.58 = (bf16[8,64,512]{2,1,0:T(8,128)(2,1)S(1)}, bf16[8,64,512]{2,1,0:T(8,128)(2,1)S(1)}, u32[]{:S(2)}, u32[]{:S(2)}) collective-permute-start(bf16[8,64,512]{2,1,0:T(8,128)(2,1)S(1)} %fusion.12), channel_id=1, source_target_pairs={{0,8},{8,16},{16,24},{24,28},{28,20},{20,12},{12,4},{4,0},{1,9},{9... | collective-permute-start | bytes 1572872 | tf_op jit(solution)/shard_map/ppermute | solution.py:52
  518.1 18.7 %collective-permute-start.50 = (bf16[1,8,64,512]{3,2,1,0:T(8,128)(2,1)S(1)}, bf16[1,8,64,512]{3,2,1,0:T(8,128)(2,1)S(1)}, u32[]{:S(2)}, u32[]{:S(2)}) collective-permute-start(bf16[1,8,64,512]{3,2,1,0:T(8,128)(2,1)S(1)} %fusion.29), channel_id=1, source_target_pairs={{0,2},{1,3},{2,0},{3,1},{4,6},{5,7},{6,4},{7,5},{8,10},{9,11},{10,... | collective-permute-start | bytes 1572872 | tf_op jit(solution)/shard_map/ppermute | solution.py:58
  (73 other events, 663.4 us)
